TPU v7x, 32 devices: a whole 2x2x4 slice. The times are simulated.
32 devices in a mesh: layer: 8 (over y, x, core), feat: 4 (over z).
Axes of the slice: x: 2, y: 2, z: 4, core: 2. Of those that a mesh axis runs over, the one named last changes fastest.
Arguments:
- tokens_in: bfloat16 [512, 4096], P('feat', 'layer'), may hold values from -6 to 6
- targets: bfloat16 [512, 4096], P('feat', 'layer'), may hold values from -6 to 6
- enc_weight: bfloat16 [2048, 32768], P(None, ('layer', 'feat')), may hold values from -0.125 to 0.125
- enc_bias: float32 [32768], P(('layer', 'feat')), may hold values from -1 to 0.5
- dec_weight: bfloat16 [2, 32768, 2048], P(None, ('layer', 'feat')), may hold values from -0.046875 to 0.046875
Outputs:
- recon_error: float32 [512, 4096], P('feat', 'layer')
- mean_square: float32 [], replicated
- enc_grad: bfloat16 [2048, 32768], P(None, ('layer', 'feat'))
- bias_grad: float32 [32768], P(('layer', 'feat'))
- dec_grad: bfloat16 [2, 32768, 2048], P(None, ('layer', 'feat'))
All inputs are finite; a program needn't handle non-finite values.
Results may differ from a plain program's by a relative error of at most 0.02.
Values may be sent and summed in bfloat16 or wider, within the bound.
No kernel may reach another device: no remote copies, remote signals or barrier semaphores. Data moves between devices by JAX's collectives and lax.ppermute only.
A program may use at most 128 MiB of HBM per device.

v0:
```python
import jax
import jax.numpy as jnp
from jax import lax
from jax.sharding import PartitionSpec as P

D = 2048
LAYERS = 2
TOK = 512


loss_scale = 64.0


def swapped(value, axis, stride):
    mask = 2**stride
    pairs = [(source, source ^ mask) for source in range(lax.axis_size(axis))]
    return lax.ppermute(value, axis, pairs)


def arrange_group(gathered, which_group, feat_count, sub_count):
    row_count = gathered.shape[1]
    col_count = gathered.shape[2]
    blocks = gathered.reshape(gathered.shape[0] // feat_count, feat_count, row_count, col_count)
    chosen = lax.dynamic_slice_in_dim(blocks, which_group * sub_count, sub_count, 0)
    return jnp.transpose(chosen, (1, 2, 0, 3)).reshape(
        feat_count * row_count, sub_count * col_count
    )


def order_pair(current, partner, member, bit_level, axis_dim):
    lower_first = member >> bit_level & 1 == 0
    leading = jnp.where(lower_first, current, partner)
    trailing = jnp.where(lower_first, partner, current)
    return jnp.concatenate([leading, trailing], axis_dim)


def on_device(tokens_in, targets, enc_weight, enc_bias, dec_weight):
    sub_count = lax.axis_size("layer") // LAYERS
    position = lax.axis_index("layer")
    layer_group = position // sub_count
    member = position % sub_count
    feat_count = lax.axis_size("feat")
    col_count = tokens_in.shape[1]
    bit_count = sub_count.bit_length() - 1
    joined = tokens_in
    for bit_level in range(bit_count):
        partner = swapped(joined, "layer", bit_level)
        joined = order_pair(joined, partner, member, bit_level, 1)
    inputs = lax.all_gather(joined, "feat", axis=0, tiled=True)
    pre_act = jnp.dot(inputs, enc_weight, preferred_element_type=jnp.float32) + enc_bias
    features = jnp.maximum(pre_act, 0.0).astype(jnp.bfloat16)
    summed_rows = lax.psum_scatter(
        jnp.einsum("tf,kfd->tkd", features, dec_weight, preferred_element_type=jnp.float32).astype(
            jnp.bfloat16
        ),
        "feat",
        scatter_dimension=0,
        tiled=True,
    ).astype(jnp.float32)
    gathered = lax.all_gather(
        summed_rows[None].astype(jnp.bfloat16), "layer", axis=0, tiled=True
    ).astype(jnp.float32)
    columns = lax.dynamic_slice_in_dim(gathered, member * col_count, col_count, 3)
    own_part = jnp.sum(
        lax.dynamic_slice_in_dim(columns, layer_group * sub_count, sub_count, 0)[:, :, 0, :], 0
    )
    prev_part = jnp.sum(
        lax.dynamic_slice_in_dim(
            columns, jnp.maximum(layer_group - 1, 0) * sub_count, sub_count, 0
        )[:, :, 1, :],
        0,
    )
    rebuilt = own_part + jnp.where(layer_group > 0, prev_part, 0.0)
    recon_error = rebuilt - targets.astype(jnp.float32)
    squares = lax.psum(jnp.sum(recon_error * recon_error), ("layer", "feat"))
    mean_square = squares / (LAYERS * TOK * D)
    scaled = (loss_scale / TOK * recon_error).astype(jnp.bfloat16)
    gathered = lax.all_gather(scaled[None], ("layer", "feat"), axis=0, tiled=True)
    own_grad = arrange_group(gathered, layer_group, feat_count, sub_count)
    next_index = jnp.minimum(layer_group + 1, LAYERS - 1)
    next_grad = arrange_group(gathered, next_index, feat_count, sub_count)
    next_grad = jnp.where(layer_group + 1 < LAYERS, next_grad, jnp.zeros_like(next_grad))
    recon_grads = jnp.stack([own_grad, next_grad], 0)
    feature_grad = jnp.einsum(
        "ktd,kfd->tf", recon_grads, dec_weight, preferred_element_type=jnp.float32
    )
    preact_grad = jnp.where(pre_act > 0.0, feature_grad, 0.0).astype(jnp.bfloat16)
    dec_grad = jnp.einsum(
        "tf,ktd->kfd", features, recon_grads, preferred_element_type=jnp.float32
    ).astype(jnp.bfloat16)
    enc_grad = lax.dot_general(
        inputs, preact_grad, (((0,), (0,)), ((), ())), preferred_element_type=jnp.float32
    ).astype(jnp.bfloat16)
    bias_grad = jnp.sum(preact_grad.astype(jnp.float32), 0)
    return (recon_error, mean_square, enc_grad, bias_grad, dec_grad)


def solution(mesh):
    placed = (
        P("feat", "layer"),
        P("feat", "layer"),
        P(None, ("layer", "feat")),
        P(("layer", "feat")),
        P(None, ("layer", "feat"), None),
    )
    return jax.shard_map(
        on_device,
        mesh=mesh,
        in_specs=placed,
        out_specs=(
            P("feat", "layer"),
            P(),
            P(None, ("layer", "feat")),
            P(("layer", "feat")),
            P(None, ("layer", "feat"), None),
        ),
        check_vma=False,
    )
```

profile of v0, /device:TPU:0, one launch (start us, length us, event | category | flops | bytes accessed | tf_op | source)
XLA Modules:
  0.0 349.7 jit_solution(5553423867299539583)
XLA Ops:
  7.2 0.0 all-gather.6.cloned.1.call-start
  7.2 0.5 collective-permute-start
  7.7 1.2 collective-permute-done
  8.9 0.9 broadcast_select_fusion.3
  9.9 2.9 collective-permute-start.1
  12.8 6.6 %collective-permute-done.1 = bf16[128,1024]{1,0:T(8,128)(2,1)S(1)} collective-permute-done((bf16[128,1024]{1,0:T(8,128)(2,1)S(1)}, bf16[128,1024]{1,0:T(8,128)(2,1)S(1)}, u32[]{:S(2)}, u32[]{:S(2)}) %collective-permute-start.1) | collective-permute-done | bytes 262176 | tf_op jit(solution)/shard_map/ppermute | solution.py:17
  19.4 0.1 broadcast_select_fusion.1
  19.5 0.8 pad_maximum_fusion
  20.4 0.0 all-gather.6.cloned.1.call-update
  20.4 0.0 copy-start.4
  20.4 0.0 reduce-scatter.2.cloned.1.call-start
  20.4 47.5 %all-gather.6.cloned.1.call-done = bf16[512,2048]{1,0:T(8,128)(2,1)} async-done(((bf16[128,2048]{1,0:T(8,128)(2,1)}), bf16[512,2048]{1,0:T(8,128)(2,1)}) %all-gather.6.cloned.1.call-update) | async-done | bytes 2097168 | tf_op jit(solution)/shard_map/all_gather | solution.py:49
  68.0 5.1 %fusion.7 = f32[512,1024]{1,0:T(8,128)S(1)} fusion(bf16[512,2048]{1,0:T(8,128)(2,1)} %all-gather.6.cloned.1.call-done, bf16[2048,1024]{1,0:T(8,128)(2,1)} %param.7), kind=kOutput, calls=%fused_computation.29 | convolution fusion | flops 2147483648 | bytes 8388608 | tf_op jit(solution)/shard_map/dot_general | solution.py:50
  73.1 0.0 copy-start.5
  73.1 1.3 copy-done.5
  74.5 0.0 copy-done.4
  74.5 9.4 %convolution_convert_fusion = bf16[512,2,2048]{2,0,1:T(8,128)(2,1)} fusion(bf16[2,1024,2048]{2,1,0:T(8,128)(2,1)} %param.9, f32[512,1024]{1,0:T(8,128)S(1)} %fusion.7, f32[1024]{0:T(1024)S(1)} %copy-done.4), kind=kOutput, calls=%fused_computation.1 | convolution fusion | flops 4298637312 | bytes 14684160 | tf_op jit(solution)/shard_map/tf,kfd->tkd/dot_general | solution.py:53
  83.9 0.0 reduce-scatter.2.cloned.1.call-update
  83.9 0.0 all-gather.8.cloned.1.call-start
  84.0 75.6 %reduce-scatter.2.cloned.1.call-done = bf16[128,2,2048]{2,0,1:T(8,128)(2,1)} async-done(((bf16[512,2,2048]{2,0,1:T(8,128)(2,1)}), bf16[128,2,2048]{2,0,1:T(8,128)(2,1)}) %reduce-scatter.2.cloned.1.call-update) | async-done | bytes 1048592 | tf_op jit(solution)/shard_map/reduce_scatter | solution.py:52
  159.6 0.0 all-gather.8.cloned.1.call-update
  159.6 0.0 all-gather.10.cloned.1.call-start
  159.7 56.9 %all-gather.8.cloned.1.call-done = bf16[1024,2,2048]{2,0,1:T(8,128)(2,1)} async-done(((bf16[128,2,2048]{2,0,1:T(8,128)(2,1)}), bf16[1024,2,2048]{2,0,1:T(8,128)(2,1)}) %all-gather.8.cloned.1.call-update) | async-done | bytes 8388624 | tf_op jit(solution)/shard_map/all_gather | solution.py:60
  216.6 11.3 %bitcast_convert_fusion = f32[8,128,2,2048]{3,1,0,2:T(8,128)} fusion(bf16[1024,2,2048]{2,0,1:T(8,128)(2,1)} %all-gather.8.cloned.1.call-done), kind=kLoop, calls=%fused_computation.26 | loop fusion | flops 4194304 | bytes 25165824 | tf_op jit(solution)/shard_map/convert_element_type | solution.py:62
  227.8 0.0 copy-start.2
  227.8 2.4 dynamic-slice_reduce_fusion
  230.2 0.0 copy-done.2
  230.2 0.7 multiply_convert_fusion
  231.0 0.0 copy-start.1
  231.0 0.0 all-gather.10.cloned.1.call-update
  231.0 0.7 multiply_reduce_fusion
  231.7 39.9 %psum.7 = f32[]{:T(128)} all-reduce(f32[]{:T(128)} %multiply_reduce_fusion), channel_id=1, replica_groups=mesh['layer'=8,'feat'=4] {'layer','feat'}, use_global_device_ids=true, to_apply=%region_4.5 | all-reduce | flops 1 | bytes 8 | tf_op jit(solution)/shard_map/psum | solution.py:75
  272.3 21.1 %all-gather.10.cloned.1.call-done = bf16[4096,512]{1,0:T(8,128)(2,1)} async-done(((bf16[128,512]{1,0:T(8,128)(2,1)}), bf16[4096,512]{1,0:T(8,128)(2,1)}) %all-gather.10.cloned.1.call-update) | async-done | bytes 4194320 | tf_op jit(solution)/shard_map/all_gather | solution.py:78
  293.4 2.5 constant_dynamic-slice_fusion
  295.9 0.0 copy-done.1
  295.9 4.1 %fusion = (bf16[4,128,4,512]{3,2,1,0:T(4,128)(2,1)}, bf16[4,128,4,512]{3,2,1,0:T(4,128)(2,1)}) fusion(bf16[4,4,128,512]{3,2,1,0:T(8,128)(2,1)S(1)} %get-tuple-element.14, pred[]{:T(512)S(6)} %lt.26, bf16[4,4,128,512]{3,2,1,0:T(8,128)(2,1)S(1)} %get-tuple-element.15), kind=kLoop, calls=%fused_computation.4 | loop fusion | flops 1048576 | bytes 8388609 | tf_op jit(solution)/shard_map/jit(_where)/select_n | solution.py:82
  300.0 3.3 stack_reshape.3
  303.3 1.5 constant_dynamic-update-slice_fusion.1
  304.7 3.3 select_n.107
  308.0 0.0 slice-start
  308.0 1.5 constant_dynamic-update-slice_fusion
  309.5 0.0 copy-start
  309.5 0.0 slice-start.1
  309.5 0.0 copy-start.6
  309.5 11.2 %convert_bitcast_fusion = bf16[2,1024,2048]{1,2,0:T(8,128)(2,1)} fusion(bf16[2,512,2048]{2,1,0:T(8,128)(2,1)} %constant_dynamic-update-slice_fusion, f32[512,1024]{1,0:T(8,128)} %copy-done.5, f32[1024]{0:T(1024)S(1)} %copy-done.4), kind=kOutput, calls=%fused_computation | convolution fusion | flops 4300734464 | bytes 14684160 | tf_op jit(solution)/shard_map/tf,ktd->kfd/dot_general | solution.py:88
  320.7 0.0 slice-done
  320.7 0.0 copy-done
  320.7 0.0 slice-done.1
  320.7 0.0 copy-done.6
  320.7 5.2 %convert_reduce_fusion = (f32[1024]{0:T(1024)}, bf16[512,1024]{1,0:T(8,128)(2,1)S(1)}) fusion(bf16[2,512,2048]{2,1,0:T(8,128)(2,1)S(1)} %copy-done, bf16[2,1024,2048]{2,1,0:T(8,128)(2,1)S(1)} %bitcast.28, f32[512,1024]{1,0:T(8,128)S(1)} %copy-done.6, f32[1024]{0:T(1024)S(1)} %copy-done.4), kind=kOutput, calls=%fused_computation.8 | convolution fusion | flops 4298112000 | bytes 15736832 | tf_op jit(solution)/shard_map/ktd,kfd->tf/dot_general | solution.py:84
  325.9 0.0 copy-start.3
  325.9 11.7 %copy.13 = bf16[2,1024,2048]{2,1,0:T(8,128)(2,1)} copy(bf16[2,1024,2048]{1,2,0:T(8,128)(2,1)} %convert_bitcast_fusion) | data formatting | bytes 16777216
  337.7 0.0 copy-done.3
  337.7 4.4 %convolution_convert_fusion.1 = bf16[2048,1024]{1,0:T(8,128)(2,1)} fusion(bf16[512,2048]{1,0:T(8,128)(2,1)S(1)} %copy-done.3, bf16[512,1024]{1,0:T(8,128)(2,1)S(1)} %get-tuple-element.21), kind=kOutput, calls=%fused_computation.2 | convolution fusion | flops 2149580800 | bytes 7340032 | tf_op jit(solution)/shard_map/dot_general | solution.py:91
  (2 shorter events, 0.0 us)
Async XLA Ops:
  7.2 60.8 %all-gather.6.cloned.1.call-start = ((), (), s32[]{:S(2)}) async-start(), calls=%async_computation.1 | async-start | bytes 2621440 | tf_op jit(solution)/shard_map/all_gather | solution.py:49
  7.2 1.7 collective-permute-start
  9.9 9.5 %collective-permute-start.1 = (bf16[128,1024]{1,0:T(8,128)(2,1)S(1)}, bf16[128,1024]{1,0:T(8,128)(2,1)S(1)}, u32[]{:S(2)}, u32[]{:S(2)}) collective-permute-start(bf16[128,1024]{1,0:T(8,128)(2,1)S(1)} %pad_maximum_fusion.1), channel_id=1, source_target_pairs={{0,8},{4,12},{8,0},{12,4},{16,24},{20,28},{24,16},{28,20},{1,9},{5... | collective-permute-start | bytes 786440 | tf_op jit(solution)/shard_map/ppermute | solution.py:17
  20.4 54.1 %copy-start.4 = (f32[1024]{0:T(1024)S(1)}, f32[1024]{0:T(1024)}, u32[]{:S(2)}) copy-start(f32[1024]{0:T(1024)} %param.8) | copy-start | bytes 12292
  20.4 139.2 %reduce-scatter.2.cloned.1.call-start = ((), (), s32[]{:S(2)}) async-start(), calls=%async_computation.2 | async-start | bytes 5242880 | tf_op jit(solution)/shard_map/reduce_scatter | solution.py:52
  73.1 1.3 copy-start.5
  83.9 132.6 %all-gather.8.cloned.1.call-start = ((), (), s32[]{:S(2)}) async-start(), calls=%async_computation.3 | async-start | bytes 9437184 | tf_op jit(solution)/shard_map/all_gather | solution.py:60
  159.6 133.8 %all-gather.10.cloned.1.call-start = ((), (), s32[]{:S(2)}) async-start(), calls=%async_computation.4 | async-start | bytes 4325376 | tf_op jit(solution)/shard_map/all_gather | solution.py:78
  227.8 2.4 copy-start.2
  231.0 64.9 %copy-start.1 = (f32[128,512]{1,0:T(8,128)}, f32[128,512]{1,0:T(8,128)S(1)}, u32[]{:S(2)}) copy-start(f32[128,512]{1,0:T(8,128)S(1)} %get-tuple-element.13) | copy-start | bytes 786436
  308.0 12.7 %slice-start = ((s8[8388608]{0:T(1024)(128)(4,1)}), s8[4194304]{0:T(1024)(128)(4,1)S(1)}, s32[]{:S(2)}) async-start(s8[8388608]{0:T(1024)(128)(4,1)} %bitcast.27), calls=%async_computation.5 | async-start | bytes 8388608
  309.5 11.2 %copy-start = (bf16[2,512,2048]{2,1,0:T(8,128)(2,1)S(1)}, bf16[2,512,2048]{2,1,0:T(8,128)(2,1)}, u32[]{:S(2)}) copy-start(bf16[2,512,2048]{2,1,0:T(8,128)(2,1)} %constant_dynamic-update-slice_fusion) | copy-start | bytes 12582916
  309.5 11.2 %slice-start.1 = ((s8[8388608]{0:T(1024)(128)(4,1)}), s8[4194304]{0:T(1024)(128)(4,1)S(1)}, s32[]{:S(2)}) async-start(s8[8388608]{0:T(1024)(128)(4,1)} %bitcast.27), calls=%async_computation.6 | async-start | bytes 8388608
  309.5 11.2 %copy-start.6 = (f32[512,1024]{1,0:T(8,128)S(1)}, f32[512,1024]{1,0:T(8,128)}, u32[]{:S(2)}) copy-start(f32[512,1024]{1,0:T(8,128)} %copy-done.5) | copy-start | bytes 6291460
  325.9 11.7 %copy-start.3 = (bf16[512,2048]{1,0:T(8,128)(2,1)S(1)}, bf16[512,2048]{1,0:T(8,128)(2,1)}, u32[]{:S(2)}) copy-start(bf16[512,2048]{1,0:T(8,128)(2,1)} %all-gather.6.cloned.1.call-done) | copy-start | bytes 6291460
Sparse Core Ops, SparseCore 0:
  20.5 47.4 all-gather.5
  84.1 75.4 reduce-scatter.1
  161.6 54.8 all-gather.7
  231.1 62.2 all-gather.9
where the time goes:
time: 350 us
  waiting for transfers between devices  209 us (60%)
  blocking collectives  39.9 us (11%)
  matrix products  35.4 us (10%)
  local copies, waits for them, and re-layouts  25 us (7%)
  other arithmetic  21 us (6%)
  between operations  15.7 us (4%)
  starting transfers between devices  3.59 us (1%)
    reduce_scatter x1, waiting for transfers between devices, on_device(): lax.psum_scatter(jnp.einsum('tf,kfd->tkd', features, dec_weight, preferre...  75.6 us
    all_gather x1, waiting for transfers between devices, on_device(): lax.all_gather(summed_rows[None].astype(jnp.bfloat16), 'layer', axis=0, t...  56.9 us
    all_gather x1, waiting for transfers between devices, on_device(): inputs = lax.all_gather(joined, 'feat', axis=0, tiled=True)  47.5 us
    psum x1, blocking collectives, on_device(): squares = lax.psum(jnp.sum(recon_error * recon_error), ('layer', 'feat'))  39.9 us
    all_gather x1, waiting for transfers between devices, on_device(): lax.all_gather(scaled[None], ('layer', 'feat'), axis=0, tiled=True)  21.1 us
    unnamed x20, local copies, waits for them, and re-layouts  14.5 us
    convert_element_type x1, other arithmetic, on_device(): gathered = lax.all_gather(summed_rows[None].astype(jnp.bfloat16), 'layer'...  11.3 us
    dot_general x1, matrix products, on_device(): jnp.einsum('tf,ktd->kfd', features, recon_grads, preferred_element_type=j...  11.2 us
  transfers between devices with their start and end apart: 6, of which 6 were waited for; matrix products, arithmetic and copies ran while one was open for 0% of the time, Pallas kernels for 0%

commit v1 on v0

v1 whole, which is shorter than its diff:
```python
import jax
import jax.numpy as jnp
from jax import lax
from jax.experimental import pallas as pl
from jax.experimental.pallas import tpu as pltpu
from jax.sharding import PartitionSpec as P

loss_scale = 64.0
vmem_limit = 50 * 1024 * 1024


def over_feat(value, mask):
    pairs = [(source, source ^ mask) for source in range(lax.axis_size("feat"))]
    return lax.ppermute(value, "feat", pairs)


def over_members(value, bit_level):
    mask = 2**bit_level
    pairs = [(source, source ^ mask) for source in range(lax.axis_size("layer"))]
    return lax.ppermute(value, "layer", pairs)


def to_layer(value, offset, sub_count):
    count = lax.axis_size("layer")
    shift = offset * sub_count
    pairs = [(p, p + shift) for p in range(count) if 0 <= p + shift < count]
    return lax.ppermute(value, "layer", pairs)


def params(flops, bytes_accessed):
    return dict(
        compiler_params=pltpu.CompilerParams(vmem_limit_bytes=vmem_limit),
        cost_estimate=pl.CostEstimate(
            flops=flops, bytes_accessed=bytes_accessed, transcendentals=0
        ),
    )


def whole(shape):
    return pl.BlockSpec(shape, lambda *_: (0,) * len(shape))


def encode_first(indices, pieces, enc_weight):
    count, feat_count, rows, cols = pieces.shape
    tok = feat_count * rows
    width = enc_weight.shape[1]

    def kernel(index_ref, piece_ref, weight_ref, out_ref):
        product = jnp.dot(
            piece_ref[0].reshape(tok, cols), weight_ref[...], preferred_element_type=jnp.float32
        )

        @pl.when(pl.program_id(0) == 0)
        def _():
            out_ref[...] = product

        @pl.when(pl.program_id(0) > 0)
        def _():
            out_ref[...] += product

    return pl.pallas_call(
        kernel,
        grid_spec=pltpu.PrefetchScalarGridSpec(
            num_scalar_prefetch=1,
            grid=(count,),
            in_specs=[
                pl.BlockSpec((1, feat_count, rows, cols), lambda i, idx: (i, 0, 0, 0)),
                pl.BlockSpec((cols, width), lambda i, idx: (idx[i], 0)),
            ],
            out_specs=whole((tok, width)),
        ),
        out_shape=jax.ShapeDtypeStruct((tok, width), jnp.float32),
        name="encode_first",
        **params(2 * count * tok * cols * width, 2 * count * cols * (tok + width) + 4 * tok * width),
    )(indices, pieces, enc_weight)


def encode_last(indices, pieces, enc_weight, partial, bias):
    count, feat_count, rows, cols = pieces.shape
    tok = feat_count * rows
    width = enc_weight.shape[1]

    def kernel(index_ref, piece_ref, weight_ref, partial_ref, bias_ref, feat_ref, mask_ref, total):
        step = pl.program_id(0)
        product = jnp.dot(
            piece_ref[0].reshape(tok, cols), weight_ref[...], preferred_element_type=jnp.float32
        )

        @pl.when(step == 0)
        def _():
            total[...] = partial_ref[...] + product

        @pl.when(step > 0)
        def _():
            total[...] += product

        @pl.when(step == count - 1)
        def _():
            pre_act = total[...] + bias_ref[...]
            feat_ref[...] = jnp.maximum(pre_act, 0.0).astype(jnp.bfloat16)
            mask_ref[...] = jnp.where(pre_act > 0.0, 1.0, 0.0).astype(jnp.bfloat16)

    return pl.pallas_call(
        kernel,
        grid_spec=pltpu.PrefetchScalarGridSpec(
            num_scalar_prefetch=1,
            grid=(count,),
            in_specs=[
                pl.BlockSpec((1, feat_count, rows, cols), lambda i, idx: (i, 0, 0, 0)),
                pl.BlockSpec((cols, width), lambda i, idx: (idx[i], 0)),
                whole((tok, width)),
                whole((1, width)),
            ],
            out_specs=[whole((tok, width)), whole((tok, width))],
            scratch_shapes=[pltpu.VMEM((tok, width), jnp.float32)],
        ),
        out_shape=[
            jax.ShapeDtypeStruct((tok, width), jnp.bfloat16),
            jax.ShapeDtypeStruct((tok, width), jnp.bfloat16),
        ],
        name="encode_last",
        **params(2 * count * tok * cols * width, 2 * count * cols * (tok + width) + 8 * tok * width),
    )(indices, pieces, enc_weight, partial, bias)


def decode(indices, features, dec_weight, offset, groups, rows, cols):
    tok, width = features.shape
    count = indices.shape[0]

    def kernel(index_ref, feat_ref, weight_ref, *out_refs):
        product = jnp.dot(feat_ref[...], weight_ref[0], preferred_element_type=jnp.float32)
        product = product.astype(jnp.bfloat16)
        for group, out_ref in zip(groups, out_refs):
            for place, block in enumerate(group):
                out_ref[0, place] = product[block * rows : (block + 1) * rows]

    return pl.pallas_call(
        kernel,
        grid_spec=pltpu.PrefetchScalarGridSpec(
            num_scalar_prefetch=1,
            grid=(count,),
            in_specs=[
                whole((tok, width)),
                pl.BlockSpec((1, width, cols), lambda i, idx: (offset, 0, idx[i])),
            ],
            out_specs=[
                pl.BlockSpec((1, len(group), rows, cols), lambda i, idx: (i, 0, 0, 0))
                for group in groups
            ],
        ),
        out_shape=[
            jax.ShapeDtypeStruct((count, len(group), rows, cols), jnp.bfloat16) for group in groups
        ],
        name="decode",
        **params(
            2 * count * tok * cols * width, 2 * count * cols * (tok + width) + 2 * tok * width
        ),
    )(indices, features, dec_weight)


def backward_piece(indices, grads, features, dec_weight, feature_grad, dec_grad):
    layers, width, depth = dec_weight.shape
    tok = features.shape[0]
    cols = grads[0][0].shape[2]
    per_layer = len(grads[0])
    flat = [piece for layer in grads for piece in layer]
    first = feature_grad is None

    def kernel(index_ref, *refs):
        grad_refs = refs[: len(flat)]
        feat_ref, weight_ref = refs[len(flat) : len(flat) + 2]
        out_ref, dec_ref = refs[-2:]
        step = pl.program_id(0)
        for k in range(layers):

            @pl.when(step == k)
            def _():
                parts = [
                    ref[...].reshape(-1, cols)
                    for ref in grad_refs[k * per_layer : (k + 1) * per_layer]
                ]
                grad = jnp.concatenate(parts, 0) if len(parts) > 1 else parts[0]
                product = lax.dot_general(
                    grad,
                    weight_ref[0],
                    (((1,), (1,)), ((), ())),
                    preferred_element_type=jnp.float32,
                )
                if k > 0:
                    out_ref[...] += product
                elif first:
                    out_ref[...] = product
                else:
                    out_ref[...] = refs[len(flat) + 2][...] + product
                dec_ref[0] = lax.dot_general(
                    feat_ref[...],
                    grad,
                    (((0,), (0,)), ((), ())),
                    preferred_element_type=jnp.float32,
                ).astype(jnp.bfloat16)

    extra_specs, extra, aliases = [], [], {}
    if not first:
        extra_specs = [whole((tok, width)), pl.BlockSpec(memory_space=pl.ANY)]
        extra = [feature_grad, dec_grad]
        aliases = {1 + len(flat) + 3: 1}
    return pl.pallas_call(
        kernel,
        grid_spec=pltpu.PrefetchScalarGridSpec(
            num_scalar_prefetch=1,
            grid=(layers,),
            in_specs=[whole(piece.shape) for piece in flat]
            + [
                whole((tok, width)),
                pl.BlockSpec((1, width, cols), lambda k, idx: (k, 0, idx[0])),
            ]
            + extra_specs,
            out_specs=[
                whole((tok, width)),
                pl.BlockSpec((1, width, cols), lambda k, idx: (k, 0, idx[0])),
            ],
        ),
        out_shape=[
            jax.ShapeDtypeStruct((tok, width), jnp.float32),
            jax.ShapeDtypeStruct((layers, width, depth), jnp.bfloat16),
        ],
        input_output_aliases=aliases,
        name="backward_piece",
        **params(
            4 * layers * tok * cols * width,
            4 * layers * cols * (tok + width) + 10 * tok * width,
        ),
    )(indices, *flat, features, dec_weight, *extra)


def encoder_grad(indices, halves, mask, feature_grad):
    count, feat_count, rows, cols = halves[0].shape
    tok, width = mask.shape

    def kernel(index_ref, low_ref, high_ref, mask_ref, grad_ref, enc_ref, bias_ref, preact):
        step = pl.program_id(0)

        @pl.when(step == 0)
        def _():
            kept = jnp.where(mask_ref[...] > 0.0, grad_ref[...], 0.0).astype(jnp.bfloat16)
            preact[...] = kept
            bias_ref[...] = jnp.sum(kept.astype(jnp.float32), 0, keepdims=True)

        for half, ref in enumerate((low_ref, high_ref)):

            @pl.when(step // count == half)
            def _():
                enc_ref[...] = lax.dot_general(
                    ref[0].reshape(tok, cols),
                    preact[...],
                    (((0,), (0,)), ((), ())),
                    preferred_element_type=jnp.float32,
                ).astype(jnp.bfloat16)

    return pl.pallas_call(
        kernel,
        grid_spec=pltpu.PrefetchScalarGridSpec(
            num_scalar_prefetch=1,
            grid=(2 * count,),
            in_specs=[
                pl.BlockSpec(
                    (1, feat_count, rows, cols),
                    lambda i, idx: (jnp.minimum(i, count - 1), 0, 0, 0),
                ),
                pl.BlockSpec(
                    (1, feat_count, rows, cols),
                    lambda i, idx: (jnp.maximum(i - count, 0), 0, 0, 0),
                ),
                whole((tok, width)),
                whole((tok, width)),
            ],
            out_specs=[
                pl.BlockSpec((cols, width), lambda i, idx: (idx[i], 0)),
                whole((1, width)),
            ],
            scratch_shapes=[pltpu.VMEM((tok, width), jnp.bfloat16)],
        ),
        out_shape=[
            jax.ShapeDtypeStruct((2 * count * cols, width), jnp.bfloat16),
            jax.ShapeDtypeStruct((1, width), jnp.float32),
        ],
        name="encoder_grad",
        **params(
            4 * count * tok * cols * width, 4 * count * cols * (tok + width) + 6 * tok * width
        ),
    )(indices, halves[0], halves[1], mask, feature_grad)


def add_pair(left, right):
    return (left.astype(jnp.float32) + right.astype(jnp.float32)).astype(jnp.bfloat16)


def on_device(tokens_in, targets, enc_weight, enc_bias, dec_weight):
    layers, width, depth = dec_weight.shape
    feat_count = lax.axis_size("feat")
    sub_count = lax.axis_size("layer") // layers
    member = lax.axis_index("layer") % sub_count
    rows, cols = tokens_in.shape
    bit_count = sub_count.bit_length() - 1
    pairs = sub_count // 2
    near = member ^ (2 * jnp.arange(pairs, dtype=jnp.int32))
    far = near ^ 1
    groups = [list(range(feat_count))]

    held = {0: [tokens_in] + [over_feat(tokens_in, s) for s in range(1, feat_count)]}
    for bit_level in range(bit_count - 1, 0, -1):
        for rel in list(held):
            held[rel ^ 2**bit_level] = [over_members(block, bit_level) for block in held[rel]]
    half = jnp.stack([jnp.stack(held[rel], 0) for rel in sorted(held)], 0)
    other = over_members(half, 0)
    partial = encode_first(near, half, enc_weight)
    features, mask = encode_last(far, other, enc_weight, partial, enc_bias[None])

    totals = [None] * layers
    for k in reversed(range(layers)):
        sent = decode(far, features, dec_weight, k, groups, rows, cols)
        kept = decode(near, features, dec_weight, k, groups, rows, cols)
        blocks = [None] * feat_count
        for place in reversed(range(len(groups))):
            current = add_pair(kept[place], over_members(sent[place], 0))
            for bit_level in range(1, bit_count):
                split = current.reshape((current.shape[0] // 2, 2) + current.shape[1:])
                current = add_pair(split[:, 0], over_members(split[:, 1], bit_level))
            for index, block in enumerate(groups[place]):
                blocks[block] = current[0, index]
        total = blocks[0].astype(jnp.float32)
        for s in range(1, feat_count):
            total = total + over_feat(blocks[s], s).astype(jnp.float32)
        totals[k] = total
    rebuilt = totals[0]
    for k in range(1, layers):
        rebuilt = rebuilt + to_layer(totals[k].astype(jnp.bfloat16), k, sub_count).astype(
            jnp.float32
        )
    recon_error = rebuilt - targets.astype(jnp.float32)
    scaled = (loss_scale / (feat_count * rows) * recon_error).astype(jnp.bfloat16)

    pieces = {}
    for k in range(layers):
        own = scaled if k == 0 else to_layer(scaled, -k, sub_count)
        blocks = [own] + [over_feat(own, s) for s in range(1, feat_count)]
        got = {0: [jnp.stack([blocks[s] for s in group], 0) for group in groups]}
        for bit_level in range(bit_count - 1, -1, -1):
            for rel in list(got):
                got[rel ^ 2**bit_level] = [over_members(part, bit_level) for part in got[rel]]
        for rel, parts in got.items():
            pieces.setdefault(rel, []).append(parts)

    squares = jnp.sum(recon_error * recon_error).reshape(1, 1)
    for s in range(feat_count.bit_length() - 1):
        squares = squares + over_feat(squares, 2**s)
    for s in range(lax.axis_size("layer").bit_length() - 1):
        squares = squares + over_members(squares, s)
    mean_square = squares[0, 0] / (layers * feat_count * rows * depth)

    feature_grad, dec_grad = None, None
    order = [rel for rel in sorted(pieces) if rel % 2 == 0]
    order += [rel for rel in sorted(pieces) if rel % 2 == 1]
    for rel in order:
        feature_grad, dec_grad = backward_piece(
            (member ^ rel).reshape(1), pieces[rel], features, dec_weight, feature_grad, dec_grad
        )
    enc_grad, bias_grad = encoder_grad(
        jnp.concatenate([near, far]), (half, other), mask, feature_grad
    )
    return (recon_error, mean_square, enc_grad, bias_grad[0], dec_grad)


def solution(mesh):
    placed = (
        P("feat", "layer"),
        P("feat", "layer"),
        P(None, ("layer", "feat")),
        P(("layer", "feat")),
        P(None, ("layer", "feat"), None),
    )
    return jax.shard_map(
        on_device,
        mesh=mesh,
        in_specs=placed,
        out_specs=(
            P("feat", "layer"),
            P(),
            P(None, ("layer", "feat")),
            P(("layer", "feat")),
            P(None, ("layer", "feat"), None),
        ),
        check_vma=False,
    )
```

time: 350 us -> 171 us (0.49)
  waiting for transfers between devices: 209 us -> 53.9 us
  Pallas kernels: 0 us -> 52.7 us
  starting transfers between devices: 3.59 us -> 53.7 us
  blocking collectives: 39.9 us -> 0 us
  matrix products: 35.4 us -> 0 us
  local copies, waits for them, and re-layouts: 25 us -> 1.48 us
  other arithmetic: 21 us -> 3.13 us
  between operations: 15.7 us -> 5.97 us
    all_gather x3 -> x0, waiting for transfers between devices: 126 us -> none  [the longest x1 56.9 us: on_device(): lax.all_gather(summed_rows[None].astype(jnp.bfloat16), 'layer', axis=0, t...]
    reduce_scatter x1 -> x0, waiting for transfers between devices: 75.6 us -> none  [on_device(): lax.psum_scatter(jnp.einsum('tf,kfd->tkd', features, dec_weight, preferre...]
    pallas_call x0 -> x11, Pallas kernels: none -> 52.7 us  [the longest x4 24.7 us: backward_piece(): pl.pallas_call(kernel, grid_spec=pltpu.PrefetchScalarGridSpec(num_scalar_...]
    ppermute x2 -> x37, starting transfers between devices: 3.43 us -> 53.7 us  [the longest x17 29.7 us: over_feat(): return lax.ppermute(value, 'feat', pairs)]
    ppermute x2 -> x37, waiting for transfers between devices: 7.82 us -> 53.9 us  [the longest x17 28.7 us: over_feat(): return lax.ppermute(value, 'feat', pairs)]
    psum x1 -> x0, blocking collectives: 39.9 us -> none  [on_device(): squares = lax.psum(jnp.sum(recon_error * recon_error), ('layer', 'feat'))]
    dot_general x5 -> x0, matrix products: 35.4 us -> none  [the longest x1 11.2 us: on_device(): jnp.einsum('tf,ktd->kfd', features, recon_grads, preferred_element_type=j...]
    unnamed x20 -> x16, local copies, waits for them, and re-layouts: 14.5 us -> 1.35 us
  transfers between devices with their start and end apart: 6 -> 37, of which waited for: 6 -> 15; matrix products, arithmetic and copies ran while one was open for 0% -> 2% of each run, Pallas kernels for 0% -> 18%
where the time goes in v1:
time: 171 us
  waiting for transfers between devices  53.9 us (32%)
  starting transfers between devices  53.7 us (31%)
  Pallas kernels  52.7 us (31%)
  between operations  5.97 us (3%)
  other arithmetic  3.13 us (2%)
    ppermute x17, starting transfers between devices, over_feat(): return lax.ppermute(value, 'feat', pairs)  29.7 us
    ppermute x17, waiting for transfers between devices, over_feat(): return lax.ppermute(value, 'feat', pairs)  28.7 us
    pallas_call x4, Pallas kernels, backward_piece(): pl.pallas_call(kernel, grid_spec=pltpu.PrefetchScalarGridSpec(num_scalar_...  24.7 us
    ppermute x18, waiting for transfers between devices, over_members(): return lax.ppermute(value, 'layer', pairs)  24.3 us
    ppermute x18, starting transfers between devices, over_members(): return lax.ppermute(value, 'layer', pairs)  19.1 us
    pallas_call x4, Pallas kernels, decode(): pl.pallas_call(kernel, grid_spec=pltpu.PrefetchScalarGridSpec(num_scalar_...  12.9 us
    pallas_call x1, Pallas kernels, encoder_grad(): pl.pallas_call(kernel, grid_spec=pltpu.PrefetchScalarGridSpec(num_scalar_...  6.85 us
    ppermute x2, starting transfers between devices, to_layer(): return lax.ppermute(value, 'layer', pairs)  4.9 us
  transfers between devices with their start and end apart: 37, of which 15 were waited for; matrix products, arithmetic and copies ran while one was open for 2% of the time, Pallas kernels for 18%

profile of v1, /device:TPU:0, one launch (start us, length us, event | category | flops | bytes accessed | tf_op | source)
XLA Modules:
  0.0 170.8 jit_solution(13706992712930416727)
XLA Ops:
  0.6 3.1 %collective-permute-start = (bf16[128,512]{1,0:T(8,128)(2,1)}, bf16[128,512]{1,0:T(8,128)(2,1)S(1)}, u32[]{:S(2)}, u32[]{:S(2)}) collective-permute-start(bf16[128,512]{1,0:T(8,128)(2,1)} %param.5), channel_id=1, source_target_pairs={{0,1},{1,0},{2,3},{3,2},{4,5},{5,4},{6,7},{7,6},{8,9},{9,8},{10,11... | collective-permute-start | bytes 393224 | tf_op jit(solution)/shard_map/ppermute | solution.py:14
  3.7 2.6 %collective-permute-start.1 = (bf16[128,512]{1,0:T(8,128)(2,1)}, bf16[128,512]{1,0:T(8,128)(2,1)S(1)}, u32[]{:S(2)}, u32[]{:S(2)}) collective-permute-start(bf16[128,512]{1,0:T(8,128)(2,1)} %param.5), channel_id=1, source_target_pairs={{0,2},{1,3},{2,0},{3,1},{4,6},{5,7},{6,4},{7,5},{8,10},{9,11},{10,... | collective-permute-start | bytes 393224 | tf_op jit(solution)/shard_map/ppermute | solution.py:14
  6.3 1.7 %collective-permute-start.3 = (bf16[128,512]{1,0:T(8,128)(2,1)}, bf16[128,512]{1,0:T(8,128)(2,1)S(1)}, u32[]{:S(2)}, u32[]{:S(2)}) collective-permute-start(bf16[128,512]{1,0:T(8,128)(2,1)} %param.5), channel_id=1, source_target_pairs={{0,8},{4,12},{8,0},{12,4},{16,24},{20,28},{24,16},{28,20},{1,9},{5... | collective-permute-start | bytes 393224 | tf_op jit(solution)/shard_map/ppermute | solution.py:20
  8.0 0.9 collective-permute-done
  9.0 1.7 %collective-permute-start.4 = (bf16[128,512]{1,0:T(8,128)(2,1)S(1)}, bf16[128,512]{1,0:T(8,128)(2,1)S(1)}, u32[]{:S(2)}, u32[]{:S(2)}) collective-permute-start(bf16[128,512]{1,0:T(8,128)(2,1)S(1)} %collective-permute-done), channel_id=1, source_target_pairs={{0,8},{4,12},{8,0},{12,4},{16,24},{20,28},{24,16},{28,20},{1,9},{5... | collective-permute-start | bytes 393224 | tf_op jit(solution)/shard_map/ppermute | solution.py:20
  10.7 6.2 %collective-permute-done.1 = bf16[128,512]{1,0:T(8,128)(2,1)S(1)} collective-permute-done((bf16[128,512]{1,0:T(8,128)(2,1)}, bf16[128,512]{1,0:T(8,128)(2,1)S(1)}, u32[]{:S(2)}, u32[]{:S(2)}) %collective-permute-start.1) | collective-permute-done | bytes 131104 | tf_op jit(solution)/shard_map/ppermute | solution.py:14
  16.9 1.5 collective-permute-start.5
  18.4 0.5 collective-permute-start.6
  18.9 1.0 maximum_bitcast_fusion
  19.9 1.9 %collective-permute-done.5 = bf16[128,512]{1,0:T(8,128)(2,1)S(1)} collective-permute-done((bf16[128,512]{1,0:T(8,128)(2,1)S(1)}, bf16[128,512]{1,0:T(8,128)(2,1)S(1)}, u32[]{:S(2)}, u32[]{:S(2)}) %collective-permute-start.5) | collective-permute-done | bytes 131104 | tf_op jit(solution)/shard_map/ppermute | solution.py:20
  21.8 1.5 collective-permute-done.6
  23.6 3.5 %encode_first.1.partial_ref = f32[512,1024]{1,0:T(8,128)S(1)} custom-call(s32[2]{0:T(128)S(1)} %multiply_xor_fusion.index_ref, bf16[2,4,128,512]{3,2,1,0:T(8,128)(2,1)S(1)} %pad_maximum_fusion.piece_ref.low_ref, bf16[2048,1024]{1,0:T(8,128)(2,1)} %weight_ref.7), custom_call_target="tpu_custom_call" | custom-call | flops 1073741824 | bytes 5242880 | tf_op jit(solution)/shard_map/encode_first/pallas_call | solution.py:61
  27.2 1.3 copy-done
  28.5 4.7 %encode_last.1 = (bf16[512,1024]{1,0:T(8,128)(2,1)S(1)}, bf16[512,1024]{1,0:T(8,128)(2,1)S(1)}) custom-call(s32[2]{0:T(128)S(1)} %broadcast_xor_fusion.index_ref, bf16[2,4,128,512]{3,2,1,0:T(8,128)(2,1)S(1)} %collective-permute-done.7.piece_ref.high_ref, bf16[2048,1024]{1,0:T(8,128)(2,1)} %weight_ref.7, f32[512,1024]{1,0:T(8,128)} %copy-done, ...), custom_call_target="tpu_custom_call" | custom-call | flops 1073741824 | bytes 7340032 | tf_op jit(solution)/shard_map/encode_last/pallas_call | solution.py:103
  33.2 3.2 %decode.7 = bf16[2,4,128,512]{3,2,1,0:T(8,128)(2,1)S(1)} custom-call(s32[2]{0:T(128)S(1)} %broadcast_xor_fusion.index_ref, bf16[512,1024]{1,0:T(8,128)(2,1)S(1)} %get-tuple-element.17.feat_ref.refs_2_, bf16[2,1024,2048]{2,1,0:T(8,128)(2,1)} %refs_3_.7), custom_call_target="tpu_custom_call" | custom-call | flops 1073741824 | bytes 4194304 | tf_op jit(solution)/shard_map/decode/pallas_call | solution.py:137
  36.5 0.5 collective-permute-start.13
  37.0 3.2 %decode.5 = bf16[2,4,128,512]{3,2,1,0:T(8,128)(2,1)S(1)} custom-call(s32[2]{0:T(128)S(1)} %broadcast_xor_fusion.index_ref, bf16[512,1024]{1,0:T(8,128)(2,1)S(1)} %get-tuple-element.17.feat_ref.refs_2_, bf16[2,1024,2048]{2,1,0:T(8,128)(2,1)} %refs_3_.7), custom_call_target="tpu_custom_call" | custom-call | flops 1073741824 | bytes 4194304 | tf_op jit(solution)/shard_map/decode/pallas_call | solution.py:137
  40.3 3.2 %decode.4 = bf16[2,4,128,512]{3,2,1,0:T(8,128)(2,1)S(1)} custom-call(s32[2]{0:T(128)S(1)} %multiply_xor_fusion.index_ref, bf16[512,1024]{1,0:T(8,128)(2,1)S(1)} %get-tuple-element.17.feat_ref.refs_2_, bf16[2,1024,2048]{2,1,0:T(8,128)(2,1)} %refs_3_.7), custom_call_target="tpu_custom_call" | custom-call | flops 1073741824 | bytes 4194304 | tf_op jit(solution)/shard_map/decode/pallas_call | solution.py:137
  43.6 3.2 %decode.6 = bf16[2,4,128,512]{3,2,1,0:T(8,128)(2,1)S(1)} custom-call(s32[2]{0:T(128)S(1)} %multiply_xor_fusion.index_ref, bf16[512,1024]{1,0:T(8,128)(2,1)S(1)} %get-tuple-element.17.feat_ref.refs_2_, bf16[2,1024,2048]{2,1,0:T(8,128)(2,1)} %refs_3_.7), custom_call_target="tpu_custom_call" | custom-call | flops 1073741824 | bytes 4194304 | tf_op jit(solution)/shard_map/decode/pallas_call | solution.py:137
  46.8 0.3 fusion.1
  47.2 1.5 collective-permute-start.14
  48.6 0.3 fusion
  49.0 0.7 collective-permute-start.9
  49.7 12.3 %collective-permute-done.14 = bf16[1,4,128,512]{3,2,1,0:T(8,128)(2,1)S(1)} collective-permute-done((bf16[1,4,128,512]{3,2,1,0:T(8,128)(2,1)S(1)}, bf16[1,4,128,512]{3,2,1,0:T(8,128)(2,1)S(1)}, u32[]{:S(2)}, u32[]{:S(2)}) %collective-permute-start.14) | collective-permute-done | bytes 524320 | tf_op jit(solution)/shard_map/ppermute | solution.py:20
  62.0 0.1 fusion.2
  62.1 0.8 collective-permute-start.15
  62.9 2.1 %collective-permute-start.16 = (bf16[128,512]{1,0:T(8,128)(2,1)S(1)}, bf16[128,512]{1,0:T(8,128)(2,1)S(1)}, u32[]{:S(2)}, u32[]{:S(2)}) collective-permute-start(bf16[128,512]{1,0:T(8,128)(2,1)S(1)} %get-tuple-element.36), channel_id=1, source_target_pairs={{0,2},{1,3},{2,0},{3,1},{4,6},{5,7},{6,4},{7,5},{8,10},{9,11},{10,... | collective-permute-start | bytes 393224 | tf_op jit(solution)/shard_map/ppermute | solution.py:14
  65.1 1.5 collective-permute-start.17
  66.6 6.2 %collective-permute-done.9 = bf16[1,4,128,512]{3,2,1,0:T(8,128)(2,1)S(1)} collective-permute-done((bf16[1,4,128,512]{3,2,1,0:T(8,128)(2,1)S(1)}, bf16[1,4,128,512]{3,2,1,0:T(8,128)(2,1)S(1)}, u32[]{:S(2)}, u32[]{:S(2)}) %collective-permute-start.9) | collective-permute-done | bytes 524320 | tf_op jit(solution)/shard_map/ppermute | solution.py:20
  72.9 0.8 collective-permute-start.10
  73.7 2.1 %collective-permute-start.11 = (bf16[128,512]{1,0:T(8,128)(2,1)S(1)}, bf16[128,512]{1,0:T(8,128)(2,1)S(1)}, u32[]{:S(2)}, u32[]{:S(2)}) collective-permute-start(bf16[128,512]{1,0:T(8,128)(2,1)S(1)} %get-tuple-element.33), channel_id=1, source_target_pairs={{0,2},{1,3},{2,0},{3,1},{4,6},{5,7},{6,4},{7,5},{8,10},{9,11},{10,... | collective-permute-start | bytes 393224 | tf_op jit(solution)/shard_map/ppermute | solution.py:14
  75.8 1.5 collective-permute-start.12
  77.5 3.4 %collective-permute-start.18 = (bf16[128,512]{1,0:T(8,128)(2,1)S(1)}, bf16[128,512]{1,0:T(8,128)(2,1)S(1)}, u32[]{:S(2)}, u32[]{:S(2)}) collective-permute-start(bf16[128,512]{1,0:T(8,128)(2,1)S(1)} %fusion.6), channel_id=1, source_target_pairs={{0,16},{4,20},{8,24},{12,28},{1,17},{5,21},{9,25},{13,29},{2,18},{... | collective-permute-start | bytes 393224 | tf_op jit(solution)/shard_map/ppermute | solution.py:27
  80.9 5.5 %collective-permute-done.11 = bf16[128,512]{1,0:T(8,128)(2,1)S(1)} collective-permute-done((bf16[128,512]{1,0:T(8,128)(2,1)S(1)}, bf16[128,512]{1,0:T(8,128)(2,1)S(1)}, u32[]{:S(2)}, u32[]{:S(2)}) %collective-permute-start.11) | collective-permute-done | bytes 131104 | tf_op jit(solution)/shard_map/ppermute | solution.py:14
  86.6 1.5 collective-permute-start.29
  88.0 2.1 %collective-permute-start.24 = (bf16[128,512]{1,0:T(8,128)(2,1)S(1)}, bf16[128,512]{1,0:T(8,128)(2,1)S(1)}, u32[]{:S(2)}, u32[]{:S(2)}) collective-permute-start(bf16[128,512]{1,0:T(8,128)(2,1)S(1)} %get-tuple-element.29), channel_id=1, source_target_pairs={{0,1},{1,0},{2,3},{3,2},{4,5},{5,4},{6,7},{7,6},{8,9},{9,8},{10,11... | collective-permute-start | bytes 393224 | tf_op jit(solution)/shard_map/ppermute | solution.py:14
  90.2 0.8 collective-permute-start.25
  90.9 1.7 collective-permute-start.26
  92.6 0.8 collective-permute-done.29
  93.4 2.1 %collective-permute-start.30 = (bf16[128,512]{1,0:T(8,128)(2,1)S(1)}, bf16[128,512]{1,0:T(8,128)(2,1)S(1)}, u32[]{:S(2)}, u32[]{:S(2)}) collective-permute-start(bf16[128,512]{1,0:T(8,128)(2,1)S(1)} %collective-permute-done.29), channel_id=1, source_target_pairs={{0,1},{1,0},{2,3},{3,2},{4,5},{5,4},{6,7},{7,6},{8,9},{9,8},{10,11... | collective-permute-start | bytes 393224 | tf_op jit(solution)/shard_map/ppermute | solution.py:14
  95.5 0.7 collective-permute-start.31
  96.2 1.7 collective-permute-start.32
  97.8 5.3 %collective-permute-done.25 = bf16[128,512]{1,0:T(8,128)(2,1)S(1)} collective-permute-done((bf16[128,512]{1,0:T(8,128)(2,1)S(1)}, bf16[128,512]{1,0:T(8,128)(2,1)S(1)}, u32[]{:S(2)}, u32[]{:S(2)}) %collective-permute-start.25) | collective-permute-done | bytes 131104 | tf_op jit(solution)/shard_map/ppermute | solution.py:14
  103.3 1.5 collective-permute-start.27
  104.8 8.4 %collective-permute-done.31 = bf16[128,512]{1,0:T(8,128)(2,1)S(1)} collective-permute-done((bf16[128,512]{1,0:T(8,128)(2,1)S(1)}, bf16[128,512]{1,0:T(8,128)(2,1)S(1)}, u32[]{:S(2)}, u32[]{:S(2)}) %collective-permute-start.31) | collective-permute-done | bytes 131104 | tf_op jit(solution)/shard_map/ppermute | solution.py:14
  113.3 1.6 collective-permute-start.33
  115.0 0.5 collective-permute-start.36
  115.5 0.7 multiply_reduce_fusion
  116.2 2.0 %collective-permute-start.19 = (f32[1,1]{1,0:T(1,128)}, f32[1,1]{1,0:T(1,128)}, u32[]{:S(2)}, u32[]{:S(2)}) collective-permute-start(f32[1,1]{1,0:T(1,128)} %bitcast.25), channel_id=1, source_target_pairs={{0,1},{1,0},{2,3},{3,2},{4,5},{5,4},{6,7},{7,6},{8,9},{9,8},{10,11... | collective-permute-start | bytes 20 | tf_op jit(solution)/shard_map/ppermute | solution.py:14
  118.1 1.8 %collective-permute-done.19 = f32[1,1]{1,0:T(1,128)} collective-permute-done((f32[1,1]{1,0:T(1,128)}, f32[1,1]{1,0:T(1,128)}, u32[]{:S(2)}, u32[]{:S(2)}) %collective-permute-start.19) | collective-permute-done | bytes 36 | tf_op jit(solution)/shard_map/ppermute | solution.py:14
  121.2 4.1 %collective-permute-start.20 = (f32[1,1]{1,0:T(1,128)}, f32[1,1]{1,0:T(1,128)}, u32[]{:S(2)}, u32[]{:S(2)}) collective-permute-start(f32[1,1]{1,0:T(1,128)} %add.64), channel_id=1, source_target_pairs={{0,2},{1,3},{2,0},{3,1},{4,6},{5,7},{6,4},{7,5},{8,10},{9,11},{10,... | collective-permute-start | bytes 20 | tf_op jit(solution)/shard_map/ppermute | solution.py:14
  125.4 0.5 collective-permute-done.20
  126.5 1.0 collective-permute-start.21
  127.5 0.3 collective-permute-done.21
  128.4 1.9 %collective-permute-start.22 = (f32[1,1]{1,0:T(1,128)}, f32[1,1]{1,0:T(1,128)}, u32[]{:S(2)}, u32[]{:S(2)}) collective-permute-start(f32[1,1]{1,0:T(1,128)} %add.66), channel_id=1, source_target_pairs={{0,8},{4,12},{8,0},{12,4},{16,24},{20,28},{24,16},{28,20},{1,9},{5... | collective-permute-start | bytes 20 | tf_op jit(solution)/shard_map/ppermute | solution.py:20
  130.3 1.8 %collective-permute-done.22 = f32[1,1]{1,0:T(1,128)} collective-permute-done((f32[1,1]{1,0:T(1,128)}, f32[1,1]{1,0:T(1,128)}, u32[]{:S(2)}, u32[]{:S(2)}) %collective-permute-start.22) | collective-permute-done | bytes 36 | tf_op jit(solution)/shard_map/ppermute | solution.py:20
  132.8 3.7 %collective-permute-start.23 = (f32[1,1]{1,0:T(1,128)}, f32[1,1]{1,0:T(1,128)}, u32[]{:S(2)}, u32[]{:S(2)}) collective-permute-start(f32[1,1]{1,0:T(1,128)} %add.67), channel_id=1, source_target_pairs={{0,16},{4,20},{8,24},{12,28},{16,0},{20,4},{24,8},{28,12},{1,17},{... | collective-permute-start | bytes 20 | tf_op jit(solution)/shard_map/ppermute | solution.py:20
  136.5 0.3 collective-permute-done.23
  137.6 0.5 collective-permute-start.34
  138.1 5.5 %backward_piece.4 = (f32[512,1024]{1,0:T(8,128)}, bf16[2,1024,2048]{2,1,0:T(8,128)(2,1)}) custom-call(s32[1]{0:T(128)} %bitcast.38.index_ref, bf16[4,128,512]{2,1,0:T(8,128)(2,1)S(1)} %pad_maximum_fusion.1.refs_0_, bf16[4,128,512]{2,1,0:T(8,128)(2,1)S(1)} %pad_maximum_fusion.2.refs_1_, bf16[512,1024]{1,0:T(8,128)(2,1)S(1)} %get-tuple-element.17.feat_ref.refs_2_, ...), custom_call_target="tpu_custom_call" | custom-call | flops 2147483648 | bytes 11534336 | tf_op jit(solution)/shard_map/backward_piece/pallas_call | solution.py:207
  143.6 6.5 %backward_piece.5 = (f32[512,1024]{1,0:T(8,128)}, bf16[2,1024,2048]{2,1,0:T(8,128)(2,1)}) custom-call(s32[1]{0:T(128)} %bitcast.37.index_ref, bf16[4,128,512]{2,1,0:T(8,128)(2,1)} %collective-permute-done.27.refs_0_, bf16[4,128,512]{2,1,0:T(8,128)(2,1)} %collective-permute-done.33.refs_1_, ...), custom_call_target="tpu_custom_call", output_to_operand_aliasing={{1}: (6, {})} | custom-call | flops 2147483648 | bytes 11534336 | tf_op jit(solution)/shard_map/backward_piece/pallas_call | solution.py:207
  150.1 6.2 %backward_piece.6 = (f32[512,1024]{1,0:T(8,128)}, bf16[2,1024,2048]{2,1,0:T(8,128)(2,1)}) custom-call(s32[1]{0:T(128)} %bitcast.36.index_ref, bf16[4,128,512]{2,1,0:T(8,128)(2,1)S(1)} %collective-permute-done.35.refs_0_, bf16[4,128,512]{2,1,0:T(8,128)(2,1)S(1)} %collective-permute-done.36.refs_1_, ...), custom_call_target="tpu_custom_call", output_to_operand_aliasing={{1}: (6, {})} | custom-call | flops 2147483648 | bytes 11534336 | tf_op jit(solution)/shard_map/backward_piece/pallas_call | solution.py:207
  156.4 6.4 %backward_piece.7 = (f32[512,1024]{1,0:T(8,128)}, bf16[2,1024,2048]{2,1,0:T(8,128)(2,1)}) custom-call(s32[1]{0:T(128)} %bitcast.27.index_ref, bf16[4,128,512]{2,1,0:T(8,128)(2,1)S(1)} %collective-permute-done.28.refs_0_, bf16[4,128,512]{2,1,0:T(8,128)(2,1)S(1)} %collective-permute-done.34.refs_1_, ...), custom_call_target="tpu_custom_call", output_to_operand_aliasing={{1}: (6, {})} | custom-call | flops 2147483648 | bytes 11534336 | tf_op jit(solution)/shard_map/backward_piece/pallas_call | solution.py:207
  162.9 6.8 %encoder_grad.1 = (bf16[2048,1024]{1,0:T(8,128)(2,1)}, f32[1,1024]{1,0:T(1,128)}) custom-call(s32[4]{0:T(128)S(1)} %pad_add_fusion.index_ref, bf16[2,4,128,512]{3,2,1,0:T(8,128)(2,1)S(1)} %pad_maximum_fusion.piece_ref.low_ref, bf16[2,4,128,512]{3,2,1,0:T(8,128)(2,1)S(1)} %copy-done.2, bf16[512,1024]{1,0:T(8,128)(2,1)S(1)} %copy-done.5, ...), custom_call_target="tpu_custom_call" | custom-call | flops 2147483648 | bytes 9437184 | tf_op jit(solution)/shard_map/encoder_grad/pallas_call | solution.py:260
  (56 shorter events, 1.2 us)
Async XLA Ops:
  0.6 8.3 %collective-permute-start = (bf16[128,512]{1,0:T(8,128)(2,1)}, bf16[128,512]{1,0:T(8,128)(2,1)S(1)}, u32[]{:S(2)}, u32[]{:S(2)}) collective-permute-start(bf16[128,512]{1,0:T(8,128)(2,1)} %param.5), channel_id=1, source_target_pairs={{0,1},{1,0},{2,3},{3,2},{4,5},{5,4},{6,7},{7,6},{8,9},{9,8},{10,11... | collective-permute-start | bytes 393224 | tf_op jit(solution)/shard_map/ppermute | solution.py:14
  3.7 13.2 %collective-permute-start.1 = (bf16[128,512]{1,0:T(8,128)(2,1)}, bf16[128,512]{1,0:T(8,128)(2,1)S(1)}, u32[]{:S(2)}, u32[]{:S(2)}) collective-permute-start(bf16[128,512]{1,0:T(8,128)(2,1)} %param.5), channel_id=1, source_target_pairs={{0,2},{1,3},{2,0},{3,1},{4,6},{5,7},{6,4},{7,5},{8,10},{9,11},{10,... | collective-permute-start | bytes 393224 | tf_op jit(solution)/shard_map/ppermute | solution.py:14
  6.3 12.1 %collective-permute-start.2 = (bf16[128,512]{1,0:T(8,128)(2,1)}, bf16[128,512]{1,0:T(8,128)(2,1)S(1)}, u32[]{:S(2)}, u32[]{:S(2)}) collective-permute-start(bf16[128,512]{1,0:T(8,128)(2,1)} %param.5), channel_id=1, source_target_pairs={{0,3},{1,2},{2,1},{3,0},{4,7},{5,6},{6,5},{7,4},{8,11},{9,10},{10,... | collective-permute-start | bytes 393224 | tf_op jit(solution)/shard_map/ppermute | solution.py:14
  6.3 13.6 %collective-permute-start.3 = (bf16[128,512]{1,0:T(8,128)(2,1)}, bf16[128,512]{1,0:T(8,128)(2,1)S(1)}, u32[]{:S(2)}, u32[]{:S(2)}) collective-permute-start(bf16[128,512]{1,0:T(8,128)(2,1)} %param.5), channel_id=1, source_target_pairs={{0,8},{4,12},{8,0},{12,4},{16,24},{20,28},{24,16},{28,20},{1,9},{5... | collective-permute-start | bytes 393224 | tf_op jit(solution)/shard_map/ppermute | solution.py:20
  9.0 10.9 %collective-permute-start.4 = (bf16[128,512]{1,0:T(8,128)(2,1)S(1)}, bf16[128,512]{1,0:T(8,128)(2,1)S(1)}, u32[]{:S(2)}, u32[]{:S(2)}) collective-permute-start(bf16[128,512]{1,0:T(8,128)(2,1)S(1)} %collective-permute-done), channel_id=1, source_target_pairs={{0,8},{4,12},{8,0},{12,4},{16,24},{20,28},{24,16},{28,20},{1,9},{5... | collective-permute-start | bytes 393224 | tf_op jit(solution)/shard_map/ppermute | solution.py:20
  16.9 5.0 %collective-permute-start.5 = (bf16[128,512]{1,0:T(8,128)(2,1)S(1)}, bf16[128,512]{1,0:T(8,128)(2,1)S(1)}, u32[]{:S(2)}, u32[]{:S(2)}) collective-permute-start(bf16[128,512]{1,0:T(8,128)(2,1)S(1)} %collective-permute-done.1), channel_id=1, source_target_pairs={{0,8},{4,12},{8,0},{12,4},{16,24},{20,28},{24,16},{28,20},{1,9},{5... | collective-permute-start | bytes 393224 | tf_op jit(solution)/shard_map/ppermute | solution.py:20
  18.4 5.0 %collective-permute-start.6 = (bf16[128,512]{1,0:T(8,128)(2,1)S(1)}, bf16[128,512]{1,0:T(8,128)(2,1)S(1)}, u32[]{:S(2)}, u32[]{:S(2)}) collective-permute-start(bf16[128,512]{1,0:T(8,128)(2,1)S(1)} %collective-permute-done.2), channel_id=1, source_target_pairs={{0,8},{4,12},{8,0},{12,4},{16,24},{20,28},{24,16},{28,20},{1,9},{5... | collective-permute-start | bytes 393224 | tf_op jit(solution)/shard_map/ppermute | solution.py:20
  23.5 5.0 %collective-permute-start.7 = (bf16[2,4,128,512]{3,2,1,0:T(8,128)(2,1)S(1)}, bf16[2,4,128,512]{3,2,1,0:T(8,128)(2,1)S(1)}, u32[]{:S(2)}, u32[]{:S(2)}) collective-permute-start(bf16[2,4,128,512]{3,2,1,0:T(8,128)(2,1)S(1)} %pad_maximum_fusion.piece_ref.low_ref), channel_id=1, source_target_pairs={{0,4},{4,0},{8,12},{12,8},{16,20},{20,16},{24,28},{28,24},{1,5},{5... | collective-permute-start | bytes 3145736 | tf_op jit(solution)/shard_map/ppermute | solution.py:20
  23.6 4.9 %copy-start.3 = (f32[1024]{0:T(1024)S(1)}, f32[1024]{0:T(1024)}, u32[]{:S(2)}) copy-start(f32[1024]{0:T(1024)} %param.8) | copy-start | bytes 12292
  27.2 1.3 copy-start
  28.5 4.7 %copy-start.1 = (bf16[2,4,128,512]{3,2,1,0:T(8,128)(2,1)}, bf16[2,4,128,512]{3,2,1,0:T(8,128)(2,1)S(1)}, u32[]{:S(2)}) copy-start(bf16[2,4,128,512]{3,2,1,0:T(8,128)(2,1)S(1)} %collective-permute-done.7.piece_ref.high_ref) | copy-start | bytes 3145732
  33.2 3.2 %copy-start.4 = (bf16[512,1024]{1,0:T(8,128)(2,1)}, bf16[512,1024]{1,0:T(8,128)(2,1)S(1)}, u32[]{:S(2)}) copy-start(bf16[512,1024]{1,0:T(8,128)(2,1)S(1)} %get-tuple-element.18.mask_ref) | copy-start | bytes 3145732
  36.5 10.3 %collective-permute-start.13 = (bf16[2,4,128,512]{3,2,1,0:T(8,128)(2,1)S(1)}, bf16[2,4,128,512]{3,2,1,0:T(8,128)(2,1)S(1)}, u32[]{:S(2)}, u32[]{:S(2)}) collective-permute-start(bf16[2,4,128,512]{3,2,1,0:T(8,128)(2,1)S(1)} %decode.7), channel_id=1, source_target_pairs={{0,4},{4,0},{8,12},{12,8},{16,20},{20,16},{24,28},{28,24},{1,5},{5... | collective-permute-start | bytes 3145736 | tf_op jit(solution)/shard_map/ppermute | solution.py:20
  40.2 8.4 %collective-permute-start.8 = (bf16[2,4,128,512]{3,2,1,0:T(8,128)(2,1)S(1)}, bf16[2,4,128,512]{3,2,1,0:T(8,128)(2,1)S(1)}, u32[]{:S(2)}, u32[]{:S(2)}) collective-permute-start(bf16[2,4,128,512]{3,2,1,0:T(8,128)(2,1)S(1)} %decode.5), channel_id=1, source_target_pairs={{0,4},{4,0},{8,12},{12,8},{16,20},{20,16},{24,28},{28,24},{1,5},{5... | collective-permute-start | bytes 3145736 | tf_op jit(solution)/shard_map/ppermute | solution.py:20
  47.2 14.8 %collective-permute-start.14 = (bf16[1,4,128,512]{3,2,1,0:T(8,128)(2,1)S(1)}, bf16[1,4,128,512]{3,2,1,0:T(8,128)(2,1)S(1)}, u32[]{:S(2)}, u32[]{:S(2)}) collective-permute-start(bf16[1,4,128,512]{3,2,1,0:T(8,128)(2,1)S(1)} %slice_bitcast_fusion), channel_id=1, source_target_pairs={{0,8},{4,12},{8,0},{12,4},{16,24},{20,28},{24,16},{28,20},{1,9},{5... | collective-permute-start | bytes 1572872 | tf_op jit(solution)/shard_map/ppermute | solution.py:20
  49.0 23.7 %collective-permute-start.9 = (bf16[1,4,128,512]{3,2,1,0:T(8,128)(2,1)S(1)}, bf16[1,4,128,512]{3,2,1,0:T(8,128)(2,1)S(1)}, u32[]{:S(2)}, u32[]{:S(2)}) collective-permute-start(bf16[1,4,128,512]{3,2,1,0:T(8,128)(2,1)S(1)} %slice_bitcast_fusion.2), channel_id=1, source_target_pairs={{0,8},{4,12},{8,0},{12,4},{16,24},{20,28},{24,16},{28,20},{1,9},{5... | collective-permute-start | bytes 1572872 | tf_op jit(solution)/shard_map/ppermute | solution.py:20
  62.1 24.3 %copy-start.7 = (bf16[128,512]{1,0:T(8,128)(2,1)S(1)}, bf16[128,512]{1,0:T(8,128)(2,1)}, u32[]{:S(2)}) copy-start(bf16[128,512]{1,0:T(8,128)(2,1)} %param.6) | copy-start | bytes 393220
  62.1 13.7 %collective-permute-start.15 = (bf16[128,512]{1,0:T(8,128)(2,1)S(1)}, bf16[128,512]{1,0:T(8,128)(2,1)S(1)}, u32[]{:S(2)}, u32[]{:S(2)}) collective-permute-start(bf16[128,512]{1,0:T(8,128)(2,1)S(1)} %get-tuple-element.34), channel_id=1, source_target_pairs={{0,1},{1,0},{2,3},{3,2},{4,5},{5,4},{6,7},{7,6},{8,9},{9,8},{10,11... | collective-permute-start | bytes 393224 | tf_op jit(solution)/shard_map/ppermute | solution.py:14
  62.9 14.5 %collective-permute-start.16 = (bf16[128,512]{1,0:T(8,128)(2,1)S(1)}, bf16[128,512]{1,0:T(8,128)(2,1)S(1)}, u32[]{:S(2)}, u32[]{:S(2)}) collective-permute-start(bf16[128,512]{1,0:T(8,128)(2,1)S(1)} %get-tuple-element.36), channel_id=1, source_target_pairs={{0,2},{1,3},{2,0},{3,1},{4,6},{5,7},{6,4},{7,5},{8,10},{9,11},{10,... | collective-permute-start | bytes 393224 | tf_op jit(solution)/shard_map/ppermute | solution.py:14
  65.1 12.3 %collective-permute-start.17 = (bf16[128,512]{1,0:T(8,128)(2,1)S(1)}, bf16[128,512]{1,0:T(8,128)(2,1)S(1)}, u32[]{:S(2)}, u32[]{:S(2)}) collective-permute-start(bf16[128,512]{1,0:T(8,128)(2,1)S(1)} %get-tuple-element.35), channel_id=1, source_target_pairs={{0,3},{1,2},{2,1},{3,0},{4,7},{5,6},{6,5},{7,4},{8,11},{9,10},{10,... | collective-permute-start | bytes 393224 | tf_op jit(solution)/shard_map/ppermute | solution.py:14
  72.9 8.0 %collective-permute-start.10 = (bf16[128,512]{1,0:T(8,128)(2,1)S(1)}, bf16[128,512]{1,0:T(8,128)(2,1)S(1)}, u32[]{:S(2)}, u32[]{:S(2)}) collective-permute-start(bf16[128,512]{1,0:T(8,128)(2,1)S(1)} %get-tuple-element.31), channel_id=1, source_target_pairs={{0,1},{1,0},{2,3},{3,2},{4,5},{5,4},{6,7},{7,6},{8,9},{9,8},{10,11... | collective-permute-start | bytes 393224 | tf_op jit(solution)/shard_map/ppermute | solution.py:14
  73.7 12.7 %collective-permute-start.11 = (bf16[128,512]{1,0:T(8,128)(2,1)S(1)}, bf16[128,512]{1,0:T(8,128)(2,1)S(1)}, u32[]{:S(2)}, u32[]{:S(2)}) collective-permute-start(bf16[128,512]{1,0:T(8,128)(2,1)S(1)} %get-tuple-element.33), channel_id=1, source_target_pairs={{0,2},{1,3},{2,0},{3,1},{4,6},{5,7},{6,4},{7,5},{8,10},{9,11},{10,... | collective-permute-start | bytes 393224 | tf_op jit(solution)/shard_map/ppermute | solution.py:14
  75.8 10.6 %collective-permute-start.12 = (bf16[128,512]{1,0:T(8,128)(2,1)S(1)}, bf16[128,512]{1,0:T(8,128)(2,1)S(1)}, u32[]{:S(2)}, u32[]{:S(2)}) collective-permute-start(bf16[128,512]{1,0:T(8,128)(2,1)S(1)} %get-tuple-element.32), channel_id=1, source_target_pairs={{0,3},{1,2},{2,1},{3,0},{4,7},{5,6},{6,5},{7,4},{8,11},{9,10},{10,... | collective-permute-start | bytes 393224 | tf_op jit(solution)/shard_map/ppermute | solution.py:14
  77.5 8.9 %collective-permute-start.18 = (bf16[128,512]{1,0:T(8,128)(2,1)S(1)}, bf16[128,512]{1,0:T(8,128)(2,1)S(1)}, u32[]{:S(2)}, u32[]{:S(2)}) collective-permute-start(bf16[128,512]{1,0:T(8,128)(2,1)S(1)} %fusion.6), channel_id=1, source_target_pairs={{0,16},{4,20},{8,24},{12,28},{1,17},{5,21},{9,25},{13,29},{2,18},{... | collective-permute-start | bytes 393224 | tf_op jit(solution)/shard_map/ppermute | solution.py:27
  86.5 57.0 %copy-start.6 = (f32[128,512]{1,0:T(8,128)}, f32[128,512]{1,0:T(8,128)S(1)}, u32[]{:S(2)}) copy-start(f32[128,512]{1,0:T(8,128)S(1)} %get-tuple-element.30) | copy-start | bytes 786436
  86.6 6.9 %collective-permute-start.29 = (bf16[128,512]{1,0:T(8,128)(2,1)S(1)}, bf16[128,512]{1,0:T(8,128)(2,1)S(1)}, u32[]{:S(2)}, u32[]{:S(2)}) collective-permute-start(bf16[128,512]{1,0:T(8,128)(2,1)S(1)} %get-tuple-element.29), channel_id=1, source_target_pairs={{16,0},{20,4},{24,8},{28,12},{17,1},{21,5},{25,9},{29,13},{18,2},{... | collective-permute-start | bytes 393224 | tf_op jit(solution)/shard_map/ppermute | solution.py:27
  88.0 8.1 %collective-permute-start.24 = (bf16[128,512]{1,0:T(8,128)(2,1)S(1)}, bf16[128,512]{1,0:T(8,128)(2,1)S(1)}, u32[]{:S(2)}, u32[]{:S(2)}) collective-permute-start(bf16[128,512]{1,0:T(8,128)(2,1)S(1)} %get-tuple-element.29), channel_id=1, source_target_pairs={{0,1},{1,0},{2,3},{3,2},{4,5},{5,4},{6,7},{7,6},{8,9},{9,8},{10,11... | collective-permute-start | bytes 393224 | tf_op jit(solution)/shard_map/ppermute | solution.py:14
  90.2 13.0 %collective-permute-start.25 = (bf16[128,512]{1,0:T(8,128)(2,1)S(1)}, bf16[128,512]{1,0:T(8,128)(2,1)S(1)}, u32[]{:S(2)}, u32[]{:S(2)}) collective-permute-start(bf16[128,512]{1,0:T(8,128)(2,1)S(1)} %get-tuple-element.29), channel_id=1, source_target_pairs={{0,2},{1,3},{2,0},{3,1},{4,6},{5,7},{6,4},{7,5},{8,10},{9,11},{10,... | collective-permute-start | bytes 393224 | tf_op jit(solution)/shard_map/ppermute | solution.py:14
  90.9 12.3 %collective-permute-start.26 = (bf16[128,512]{1,0:T(8,128)(2,1)S(1)}, bf16[128,512]{1,0:T(8,128)(2,1)S(1)}, u32[]{:S(2)}, u32[]{:S(2)}) collective-permute-start(bf16[128,512]{1,0:T(8,128)(2,1)S(1)} %get-tuple-element.29), channel_id=1, source_target_pairs={{0,3},{1,2},{2,1},{3,0},{4,7},{5,6},{6,5},{7,4},{8,11},{9,10},{10,... | collective-permute-start | bytes 393224 | tf_op jit(solution)/shard_map/ppermute | solution.py:14
  93.4 11.4 %collective-permute-start.30 = (bf16[128,512]{1,0:T(8,128)(2,1)S(1)}, bf16[128,512]{1,0:T(8,128)(2,1)S(1)}, u32[]{:S(2)}, u32[]{:S(2)}) collective-permute-start(bf16[128,512]{1,0:T(8,128)(2,1)S(1)} %collective-permute-done.29), channel_id=1, source_target_pairs={{0,1},{1,0},{2,3},{3,2},{4,5},{5,4},{6,7},{7,6},{8,9},{9,8},{10,11... | collective-permute-start | bytes 393224 | tf_op jit(solution)/shard_map/ppermute | solution.py:14
  95.5 17.8 %collective-permute-start.31 = (bf16[128,512]{1,0:T(8,128)(2,1)S(1)}, bf16[128,512]{1,0:T(8,128)(2,1)S(1)}, u32[]{:S(2)}, u32[]{:S(2)}) collective-permute-start(bf16[128,512]{1,0:T(8,128)(2,1)S(1)} %collective-permute-done.29), channel_id=1, source_target_pairs={{0,2},{1,3},{2,0},{3,1},{4,6},{5,7},{6,4},{7,5},{8,10},{9,11},{10,... | collective-permute-start | bytes 393224 | tf_op jit(solution)/shard_map/ppermute | solution.py:14
  96.2 17.1 %collective-permute-start.32 = (bf16[128,512]{1,0:T(8,128)(2,1)S(1)}, bf16[128,512]{1,0:T(8,128)(2,1)S(1)}, u32[]{:S(2)}, u32[]{:S(2)}) collective-permute-start(bf16[128,512]{1,0:T(8,128)(2,1)S(1)} %collective-permute-done.29), channel_id=1, source_target_pairs={{0,3},{1,2},{2,1},{3,0},{4,7},{5,6},{6,5},{7,4},{8,11},{9,10},{10,... | collective-permute-start | bytes 393224 | tf_op jit(solution)/shard_map/ppermute | solution.py:14
  103.3 34.2 %collective-permute-start.27 = (bf16[4,128,512]{2,1,0:T(8,128)(2,1)S(1)}, bf16[4,128,512]{2,1,0:T(8,128)(2,1)}, u32[]{:S(2)}, u32[]{:S(2)}) collective-permute-start(bf16[4,128,512]{2,1,0:T(8,128)(2,1)S(1)} %pad_maximum_fusion.1.refs_0_), channel_id=1, source_target_pairs={{0,8},{4,12},{8,0},{12,4},{16,24},{20,28},{24,16},{28,20},{1,9},{5... | collective-permute-start | bytes 1572872 | tf_op jit(solution)/shard_map/ppermute | solution.py:20
  113.3 24.3 %collective-permute-start.33 = (bf16[4,128,512]{2,1,0:T(8,128)(2,1)S(1)}, bf16[4,128,512]{2,1,0:T(8,128)(2,1)}, u32[]{:S(2)}, u32[]{:S(2)}) collective-permute-start(bf16[4,128,512]{2,1,0:T(8,128)(2,1)S(1)} %pad_maximum_fusion.2.refs_1_), channel_id=1, source_target_pairs={{0,8},{4,12},{8,0},{12,4},{16,24},{20,28},{24,16},{28,20},{1,9},{5... | collective-permute-start | bytes 1572872 | tf_op jit(solution)/shard_map/ppermute | solution.py:20
  115.0 35.2 %collective-permute-start.35 = (bf16[4,128,512]{2,1,0:T(8,128)(2,1)S(1)}, bf16[4,128,512]{2,1,0:T(8,128)(2,1)S(1)}, u32[]{:S(2)}, u32[]{:S(2)}) collective-permute-start(bf16[4,128,512]{2,1,0:T(8,128)(2,1)S(1)} %pad_maximum_fusion.1.refs_0_), channel_id=1, source_target_pairs={{0,4},{4,0},{8,12},{12,8},{16,20},{20,16},{24,28},{28,24},{1,5},{5... | collective-permute-start | bytes 1572872 | tf_op jit(solution)/shard_map/ppermute | solution.py:20
  115.0 35.1 %collective-permute-start.36 = (bf16[4,128,512]{2,1,0:T(8,128)(2,1)S(1)}, bf16[4,128,512]{2,1,0:T(8,128)(2,1)S(1)}, u32[]{:S(2)}, u32[]{:S(2)}) collective-permute-start(bf16[4,128,512]{2,1,0:T(8,128)(2,1)S(1)} %pad_maximum_fusion.2.refs_1_), channel_id=1, source_target_pairs={{0,4},{4,0},{8,12},{12,8},{16,20},{20,16},{24,28},{28,24},{1,5},{5... | collective-permute-start | bytes 1572872 | tf_op jit(solution)/shard_map/ppermute | solution.py:20
  116.2 3.8 %collective-permute-start.19 = (f32[1,1]{1,0:T(1,128)}, f32[1,1]{1,0:T(1,128)}, u32[]{:S(2)}, u32[]{:S(2)}) collective-permute-start(f32[1,1]{1,0:T(1,128)} %bitcast.25), channel_id=1, source_target_pairs={{0,1},{1,0},{2,3},{3,2},{4,5},{5,4},{6,7},{7,6},{8,9},{9,8},{10,11... | collective-permute-start | bytes 20 | tf_op jit(solution)/shard_map/ppermute | solution.py:14
  121.2 4.6 %collective-permute-start.20 = (f32[1,1]{1,0:T(1,128)}, f32[1,1]{1,0:T(1,128)}, u32[]{:S(2)}, u32[]{:S(2)}) collective-permute-start(f32[1,1]{1,0:T(1,128)} %add.64), channel_id=1, source_target_pairs={{0,2},{1,3},{2,0},{3,1},{4,6},{5,7},{6,4},{7,5},{8,10},{9,11},{10,... | collective-permute-start | bytes 20 | tf_op jit(solution)/shard_map/ppermute | solution.py:14
  126.5 1.3 collective-permute-start.21
  128.4 3.7 %collective-permute-start.22 = (f32[1,1]{1,0:T(1,128)}, f32[1,1]{1,0:T(1,128)}, u32[]{:S(2)}, u32[]{:S(2)}) collective-permute-start(f32[1,1]{1,0:T(1,128)} %add.66), channel_id=1, source_target_pairs={{0,8},{4,12},{8,0},{12,4},{16,24},{20,28},{24,16},{28,20},{1,9},{5... | collective-permute-start | bytes 20 | tf_op jit(solution)/shard_map/ppermute | solution.py:20
  132.8 4.1 %collective-permute-start.23 = (f32[1,1]{1,0:T(1,128)}, f32[1,1]{1,0:T(1,128)}, u32[]{:S(2)}, u32[]{:S(2)}) collective-permute-start(f32[1,1]{1,0:T(1,128)} %add.67), channel_id=1, source_target_pairs={{0,16},{4,20},{8,24},{12,28},{16,0},{20,4},{24,8},{28,12},{1,17},{... | collective-permute-start | bytes 20 | tf_op jit(solution)/shard_map/ppermute | solution.py:20
  137.5 18.9 %collective-permute-start.28 = (bf16[4,128,512]{2,1,0:T(8,128)(2,1)}, bf16[4,128,512]{2,1,0:T(8,128)(2,1)S(1)}, u32[]{:S(2)}, u32[]{:S(2)}) collective-permute-start(bf16[4,128,512]{2,1,0:T(8,128)(2,1)} %collective-permute-done.27.refs_0_), channel_id=1, source_target_pairs={{0,4},{4,0},{8,12},{12,8},{16,20},{20,16},{24,28},{28,24},{1,5},{5... | collective-permute-start | bytes 1572872 | tf_op jit(solution)/shard_map/ppermute | solution.py:20
  137.6 18.8 %collective-permute-start.34 = (bf16[4,128,512]{2,1,0:T(8,128)(2,1)}, bf16[4,128,512]{2,1,0:T(8,128)(2,1)S(1)}, u32[]{:S(2)}, u32[]{:S(2)}) collective-permute-start(bf16[4,128,512]{2,1,0:T(8,128)(2,1)} %collective-permute-done.33.refs_1_), channel_id=1, source_target_pairs={{0,4},{4,0},{8,12},{12,8},{16,20},{20,16},{24,28},{28,24},{1,5},{5... | collective-permute-start | bytes 1572872 | tf_op jit(solution)/shard_map/ppermute | solution.py:20
  156.4 6.5 %copy-start.2 = (bf16[2,4,128,512]{3,2,1,0:T(8,128)(2,1)S(1)}, bf16[2,4,128,512]{3,2,1,0:T(8,128)(2,1)}, u32[]{:S(2)}) copy-start(bf16[2,4,128,512]{3,2,1,0:T(8,128)(2,1)} %copy-done.1) | copy-start | bytes 3145732
  156.4 6.4 %copy-start.5 = (bf16[512,1024]{1,0:T(8,128)(2,1)S(1)}, bf16[512,1024]{1,0:T(8,128)(2,1)}, u32[]{:S(2)}) copy-start(bf16[512,1024]{1,0:T(8,128)(2,1)} %copy-done.4) | copy-start | bytes 3145732
